TPU v7x, 32 devices: a whole 2x2x4 slice. The times are simulated.
32 devices in a mesh: group: 2 (over x), lat: 16 (over z, y, core).
Axes of the slice: x: 2, y: 2, z: 4, core: 2. Of those that a mesh axis runs over, the one named last changes fastest.
Arguments:
- currents: float32 [16, 2, 512, 512], P('group', None, 'lat'), parts along dimension 0, may hold values from -6 to 6
- green: float32 [16, 8, 2, 1024, 1024], P('group', None, None, 'lat'), parts along dimension 0, may hold values from -5 to 5
- section_map: int32 [16], P('group'), parts along dimension 0, may hold values from 0 to 7
- offsets: int32 [16], P('group'), parts along dimension 0, may hold values from 0 to 512
Outputs:
- fields: float32 [16, 2, 512, 512], P('group', None, 'lat'), parts along dimension 0
There are 2 independent parts, one for each index of `group`. A program takes and returns all parts, laid end to end along the dimension named above; each array names one. Nothing has to cross between parts.
All inputs are finite; a program needn't handle non-finite values.
Results may differ from a plain program's by a relative error of at most 0.0003.
Values sent between devices are 32-bit elements; how exact they have to be, the bound alone decides.
A program may use at most 128 MiB of HBM per device.

v0:
```python
import functools
import math

import jax
import jax.numpy as jnp
import ml_dtypes
import numpy as np
from jax import lax
from jax.experimental import pallas as pl
from jax.experimental.pallas import tpu as pltpu
from jax.sharding import PartitionSpec as P

LANES = 128
MESH = pl.DeviceIdType.MESH


def split_np(table):
    high = table.astype(ml_dtypes.bfloat16)
    low = (table - high.astype(np.float64)).astype(ml_dtypes.bfloat16)
    return np.stack([high, low])


def waves(width, period):
    angle = 2.0 * np.pi / period * (np.arange(width)[:, None] * np.arange(period)[None, :] % period)
    return np.cos(angle), np.sin(angle)


def blocked_table(width, period, block):
    cosine, sine = waves(width, period)
    parts = [cosine.reshape(width, -1, 1, block), -sine.reshape(width, -1, 1, block)]
    return np.concatenate(parts, axis=2).reshape(width, 2 * period)


def split_bf16(values):
    high = values.astype(jnp.bfloat16)
    low = (values - high.astype(jnp.float32)).astype(jnp.bfloat16)
    return high, low


def dot32(left, right):
    return jnp.dot(left, right, preferred_element_type=jnp.float32)


def dot_split(stacked, high_table, low_table):
    rows = stacked.shape[0] // 2
    both = dot32(stacked, high_table)
    return both[:rows] + both[rows:] + dot32(stacked[:rows], low_table)


def swap_halves(values):
    half = LANES // 2
    parts = []
    for start in range(0, values.shape[-1], LANES):
        parts.append(pltpu.roll(values[:, start : start + LANES], half, 1))
    return jnp.concatenate(parts, axis=1) if len(parts) > 1 else parts[0]


def section_slots(map_ref, depths, sections):
    used = []
    for section in range(sections):
        found = map_ref[0] == section
        for depth in range(1, depths):
            found = jnp.logical_or(found, map_ref[depth] == section)
        used.append(found.astype(jnp.int32))
    rank, before = [], jnp.int32(0)
    for section in range(sections):
        rank.append(before)
        before = before + used[section]
    return rank, used


def slot_of_depth(map_ref, rank, depth):
    value = jnp.int32(0)
    for section, place in enumerate(rank):
        value = jnp.where(map_ref[depth] == section, place, value)
    return value


def forward_kernel(map_ref, cur_ref, high_ref, low_ref, cos_ref, sin_ref, out_ref, split_ref):
    depths, _, rows, width = cur_ref.shape
    sections = out_ref.shape[0]
    half = depths * rows

    @pl.when(pl.program_id(0) == 0)
    def _():
        for part in range(2):
            high, low = split_bf16(cur_ref[:, part].reshape(half, width))
            split_ref[pl.ds(part * half, half), :] = high
            split_ref[pl.ds((2 + part) * half, half), :] = low

    product = dot_split(split_ref[...], high_ref[...], low_ref[...])
    lane = lax.broadcasted_iota(jnp.int32, (1, product.shape[1]), 1) % LANES
    sign = jnp.where(lane < LANES // 2, -1.0, 1.0)
    spectrum = product[:half] + swap_halves(product[half:]) * sign
    swapped = swap_halves(spectrum)
    rank, _ = section_slots(map_ref, depths, sections)
    out_ref[...] = jnp.zeros_like(out_ref)
    for depth in range(depths):
        span = slice(depth * rows, (depth + 1) * rows)
        turned = (
            spectrum[span] * cos_ref[pl.ds(depth, 1), :]
            + swapped[span] * sin_ref[pl.ds(depth, 1), :]
        )
        out_ref[slot_of_depth(map_ref, rank, depth)] += turned


def inverse_kernel(map_ref, ret_ref, high_ref, low_ref, cos_ref, sin_ref, out_ref, split_ref):
    depths, _, rows, width = out_ref.shape
    sections = ret_ref.shape[0]
    half = depths * rows
    lanes = ret_ref.shape[2]

    @pl.when(pl.program_id(0) == 0)
    def _():
        rank, _ = section_slots(map_ref, depths, sections)
        lane = lax.broadcasted_iota(jnp.int32, (1, lanes), 1) % LANES
        sign = jnp.where(lane < LANES // 2, 1.0, -1.0)
        for depth in range(depths):
            plane = ret_ref[slot_of_depth(map_ref, rank, depth)]
            turned = (
                plane * cos_ref[pl.ds(depth, 1), :]
                - swap_halves(plane) * sin_ref[pl.ds(depth, 1), :]
            )
            crossed = swap_halves(turned) * sign
            for part, values in enumerate((turned, crossed)):
                high, low = split_bf16(values)
                split_ref[pl.ds(part * half + depth * rows, rows), :] = high
                split_ref[pl.ds((2 + part) * half + depth * rows, rows), :] = low

    product = dot_split(split_ref[...], high_ref[...], low_ref[...])
    scale = 4.0 / (lanes * lanes)
    for part in range(2):
        out_ref[:, part] = (product[part * half : (part + 1) * half] * scale).reshape(
            depths, rows, width
        )


def exchange_kernel(
    n, slots, map_ref, src_ref, green_hbm, table_hbm, back_hbm, out_ref,
    recv, green, table, back, spectra, total, result,
    send_sem, recv_sem, send_back, recv_back, load_sem, green_sem,
):
    group = lax.axis_index("group")
    me = lax.axis_index("lat")
    rows = src_ref.shape[1]
    sections, block, period = green.shape[0], green.shape[3], green.shape[4]
    width = recv.shape[1]
    tables_in = pltpu.make_async_copy(table_hbm, table, load_sem.at[0])
    back_in = pltpu.make_async_copy(back_hbm, back, load_sem.at[1])
    green_in = pltpu.make_async_copy(green_hbm, green, green_sem)
    tables_in.start()

    barrier = pltpu.get_barrier_semaphore()

    def greet(step, carry):
        other = lax.rem(me + step, n)
        pl.semaphore_signal(barrier, inc=1, device_id=(group, other), device_id_type=MESH)
        return carry

    lax.fori_loop(1, n, greet, 0)
    pl.semaphore_wait(barrier, n - 1)

    my_rows = pl.ds(pl.multiple_of(me * rows, rows), rows)
    my_lanes = pl.ds(pl.multiple_of(me * LANES, LANES), LANES)

    def send_sources(base, count):
        batch = pl.ds(base, count)
        pltpu.make_async_copy(
            src_ref.at[batch, :, my_lanes], recv.at[batch, my_rows], recv_sem.at[base // 2]
        ).start()

        def send(step, carry):
            other = lax.rem(me + step, n)
            pltpu.make_async_remote_copy(
                src_ref=src_ref.at[batch, :, pl.ds(pl.multiple_of(other * LANES, LANES), LANES)],
                dst_ref=recv.at[batch, my_rows],
                send_sem=send_sem,
                recv_sem=recv_sem.at[base // 2],
                device_id=(group, other),
                device_id_type=MESH,
            ).start()
            return carry

        lax.fori_loop(1, n, send, 0)

    def send_results(base, count):
        batch = pl.ds(base, count)
        pltpu.make_async_copy(
            result.at[batch, my_rows], out_ref.at[batch, :, my_lanes], recv_back
        ).start()

        def send(step, carry):
            other = lax.rem(me + step, n)
            pltpu.make_async_remote_copy(
                src_ref=result.at[batch, pl.ds(pl.multiple_of(other * rows, rows), rows)],
                dst_ref=out_ref.at[batch, :, my_lanes],
                send_sem=send_back,
                recv_sem=recv_back,
                device_id=(group, other),
                device_id_type=MESH,
            ).start()
            return carry

        lax.fori_loop(1, n, send, 0)

    def batches(body):
        def pair(index, carry):
            body(index * 2, 2)
            return carry

        lax.fori_loop(0, slots // 2, pair, 0)
        if slots % 2:
            body(slots - 1, 1)

    batches(send_sources)
    green_in.start()
    back_in.start()

    rank, used = section_slots(map_ref, map_ref.shape[0], sections)
    place = []
    for slot in range(slots):
        found = jnp.int32(0)
        for section in range(sections):
            here = jnp.logical_and(rank[section] == slot, used[section] == 1)
            found = jnp.where(here, section, found)
        place.append(found)

    def place_of(slot):
        found = place[0]
        for index in range(1, slots):
            found = jnp.where(slot == index, place[index], found)
        return found

    total[...] = jnp.zeros_like(total)
    tables_in.wait()
    chunk = 2 * LANES

    def take(base, count):
        arrived = recv.at[pl.ds(base, count)]
        pltpu.make_async_copy(arrived, arrived, recv_sem.at[base // 2]).wait()
        halves = [jnp.transpose(recv[base + index]) for index in range(count)]
        stacked = jnp.concatenate(halves, axis=0) if count > 1 else halves[0]
        high, low = split_bf16(stacked)
        stacked = jnp.concatenate([high, low], axis=0)

        def columns(index, carry):
            span = pl.ds(pl.multiple_of(index * chunk, chunk), chunk)
            by_cos = dot_split(stacked, table[0, 0, :, span], table[0, 1, :, span])
            by_sin = dot_split(stacked, table[1, 0, :, span], table[1, 1, :, span])
            for slot in range(count):
                real = slice(slot * 2 * block, slot * 2 * block + block)
                imag = slice(slot * 2 * block + block, (slot + 1) * 2 * block)
                spectra[slot, 0, :, span] = by_cos[real] + by_sin[imag]
                spectra[slot, 1, :, span] = by_cos[imag] - by_sin[real]
            return carry

        lax.fori_loop(0, period // chunk, columns, 0)

        @pl.when(base == 0)
        def _():
            green_in.wait()

        froms = [place_of(base + index) for index in range(count)]

        def couple(index, carry):
            span = pl.ds(pl.multiple_of(index * 8, 8), 8)
            source = [(spectra[i, 0, span, :], spectra[i, 1, span, :]) for i in range(count)]
            for slot in range(slots):
                real = total[slot, 0, span, :]
                imag = total[slot, 1, span, :]
                for i in range(count):
                    green_real = green[place[slot], froms[i], 0, span, :]
                    green_imag = green[place[slot], froms[i], 1, span, :]
                    real = real + green_real * source[i][0] - green_imag * source[i][1]
                    imag = imag + green_real * source[i][1] + green_imag * source[i][0]
                total[slot, 0, span, :] = real
                total[slot, 1, span, :] = imag
            return carry

        lax.fori_loop(0, block // 8, couple, 0)

    batches(take)
    back_in.wait()

    def give(base, count):
        stacked = total[pl.ds(base, count)].reshape(count * 2 * block, period)
        high, low = split_bf16(stacked)
        stacked = jnp.concatenate([high, low], axis=0)

        def columns(index, carry):
            span = pl.ds(pl.multiple_of(index * chunk, chunk), chunk)
            by_cos = dot_split(stacked, back[0, 0, :, span], back[0, 1, :, span])
            by_sin = dot_split(stacked, back[1, 0, :, span], back[1, 1, :, span])
            for slot in range(count):
                real = slice(slot * 2 * block, slot * 2 * block + block)
                imag = slice(slot * 2 * block + block, (slot + 1) * 2 * block)
                plane = jnp.concatenate(
                    [by_cos[real] - by_sin[imag], by_cos[imag] + by_sin[real]], axis=0
                )
                result[base + slot, span, :] = jnp.transpose(plane)
            return carry

        lax.fori_loop(0, width // chunk, columns, 0)
        send_results(base, count)

    batches(give)
    landed = out_ref.at[pl.ds(0, slots)]
    pltpu.make_async_copy(landed, landed, recv_back).wait()
    left = src_ref.at[pl.ds(0, slots), :, pl.ds(LANES, (n - 1) * LANES)]
    pltpu.make_async_copy(left, left, send_sem).wait()
    gone = result.at[pl.ds(0, slots), pl.ds(rows, width - rows)]
    pltpu.make_async_copy(gone, gone, send_back).wait()


def per_device_kernels(n, currents, green, section_map, offsets):
    depths, _, rows, width = currents.shape
    sections, _, _, block, period = green.shape
    lanes = 2 * period
    f32, bf16 = jnp.float32, jnp.bfloat16
    cosine, sine = waves(width, period)
    blocked = blocked_table(width, period, block)
    spread = jnp.asarray(split_np(blocked))
    gather = jnp.asarray(split_np(np.ascontiguousarray(blocked.T)))
    table = jnp.asarray(np.stack([split_np(cosine), split_np(sine)]))
    back = jnp.asarray(np.stack([split_np(np.ascontiguousarray(cosine.T)),
                                 split_np(np.ascontiguousarray(sine.T))]))
    lane = lax.iota(jnp.int32, lanes)
    wavenumber = lane // (2 * block) * block + lane % block
    angles = 2.0 * math.pi / period * (offsets[:, None] * wavenumber[None, :] % period).astype(f32)
    turn_cos = jnp.cos(angles)
    turn_sin = jnp.sin(angles) * jnp.where(lane % (2 * block) < block, 1.0, -1.0)
    limit = 60 * 2**20
    smem = pl.BlockSpec(memory_space=pltpu.SMEM)
    anywhere = pl.BlockSpec(memory_space=pl.ANY)
    column = 2 * LANES
    sources = pl.pallas_call(
        forward_kernel,
        grid=(lanes // column,),
        out_shape=jax.ShapeDtypeStruct((sections, rows, lanes), f32),
        in_specs=[
            smem,
            pl.BlockSpec((depths, 2, rows, width), lambda i: (0, 0, 0, 0)),
            pl.BlockSpec((None, width, column), lambda i: (0, 0, i)),
            pl.BlockSpec((None, width, column), lambda i: (1, 0, i)),
            pl.BlockSpec((depths, column), lambda i: (0, i)),
            pl.BlockSpec((depths, column), lambda i: (0, i)),
        ],
        out_specs=pl.BlockSpec((sections, rows, column), lambda i: (0, 0, i)),
        scratch_shapes=[pltpu.VMEM((4 * depths * rows, width), bf16)],
        compiler_params=pltpu.CompilerParams(vmem_limit_bytes=32 * 2**20),
    )(section_map, currents, spread, spread, turn_cos, turn_sin)

    def exchange(slots):
        return pl.pallas_call(
            functools.partial(exchange_kernel, n, slots),
            out_shape=jax.ShapeDtypeStruct((sections, rows, lanes), f32),
            in_specs=[smem] + [anywhere] * 4,
            out_specs=anywhere,
            scratch_shapes=[
                pltpu.VMEM((slots, width, LANES), f32),
                pltpu.VMEM(green.shape, f32),
                pltpu.VMEM(table.shape, bf16),
                pltpu.VMEM(back.shape, bf16),
                pltpu.VMEM((2, 2, block, period), f32),
                pltpu.VMEM((slots, 2, block, period), f32),
                pltpu.VMEM((slots, width, LANES), f32),
                pltpu.SemaphoreType.DMA,
                pltpu.SemaphoreType.DMA(((slots + 1) // 2,)),
                pltpu.SemaphoreType.DMA,
                pltpu.SemaphoreType.DMA,
                pltpu.SemaphoreType.DMA((2,)),
                pltpu.SemaphoreType.DMA,
            ],
            compiler_params=pltpu.CompilerParams(
                collective_id=slots, has_side_effects=True, vmem_limit_bytes=limit
            ),
        )

    returned = exchange(sections)(section_map, sources, green, table, back)
    return pl.pallas_call(
        inverse_kernel,
        grid=(width // column,),
        out_shape=jax.ShapeDtypeStruct(currents.shape, f32),
        in_specs=[
            smem,
            pl.BlockSpec((sections, rows, lanes), lambda i: (0, 0, 0)),
            pl.BlockSpec((None, lanes, column), lambda i: (0, 0, i)),
            pl.BlockSpec((None, lanes, column), lambda i: (1, 0, i)),
            pl.BlockSpec((depths, lanes), lambda i: (0, 0)),
            pl.BlockSpec((depths, lanes), lambda i: (0, 0)),
        ],
        out_specs=pl.BlockSpec((depths, 2, rows, column), lambda i: (0, 0, 0, i)),
        scratch_shapes=[pltpu.VMEM((4 * depths * rows, lanes), bf16)],
        compiler_params=pltpu.CompilerParams(vmem_limit_bytes=40 * 2**20),
    )(section_map, returned, gather, gather, turn_cos, turn_sin)


def dft_table(n_in, n_out, period, sign_value):
    row_ids = lax.iota(jnp.int32, n_in)
    col_ids = lax.iota(jnp.int32, n_out)
    angles = (
        2.0 * math.pi / period * (row_ids[:, None] * col_ids[None, :] % period).astype(jnp.float32)
    )
    cosine = jnp.cos(angles)
    sine_part = sign_value * jnp.sin(angles)
    return jnp.stack(
        [jnp.stack([cosine, sine_part], axis=1), jnp.stack([-sine_part, cosine], axis=1)], axis=0
    )


def phases(offsets, period, sign_value):
    col_ids = lax.iota(jnp.int32, period)
    angles = (
        2.0 * math.pi / period * (offsets[:, None] * col_ids[None, :] % period).astype(jnp.float32)
    )
    return (jnp.cos(angles)[:, None, :], sign_value * jnp.sin(angles)[:, None, :])


def rotate(planes, cosine, sine_part):
    real_part = planes[:, 0] * cosine - planes[:, 1] * sine_part
    imag_part = planes[:, 0] * sine_part + planes[:, 1] * cosine
    return jnp.stack([real_part, imag_part], axis=1)


def per_device(currents, green, section_map, offsets):
    highest = lax.Precision.HIGHEST
    plane_width = currents.shape[3]
    padded = 2 * plane_width
    sections = green.shape[0]
    forward = dft_table(plane_width, padded, padded, -1.0)
    inverse = dft_table(padded, plane_width, padded, 1.0)
    onehot = (section_map[:, None] == lax.iota(jnp.int32, sections)[None, :]).astype(jnp.float32)
    spec_y = jnp.einsum("jcxy,cydk->jdxk", currents, forward, precision=highest)
    cos_fwd, sin_fwd = phases(offsets, padded, -1.0)
    shifted = jnp.transpose(rotate(spec_y, cos_fwd, sin_fwd), (0, 2, 1, 3))
    grouped = jnp.einsum("js,jxdk->sxdk", onehot, shifted, precision=highest)
    spectra = jnp.einsum(
        "mxcq,cxdk->mdqk",
        lax.all_to_all(grouped, "lat", split_axis=3, concat_axis=1, tiled=True),
        forward,
        precision=highest,
    )
    green_real = green[:, :, 0]
    green_imag = green[:, :, 1]
    out_real = jnp.einsum(
        "tsqk,sqk->tqk", green_real, spectra[:, 0], precision=highest
    ) - jnp.einsum("tsqk,sqk->tqk", green_imag, spectra[:, 1], precision=highest)
    out_imag = jnp.einsum(
        "tsqk,sqk->tqk", green_real, spectra[:, 1], precision=highest
    ) + jnp.einsum("tsqk,sqk->tqk", green_imag, spectra[:, 0], precision=highest)
    coupled = jnp.stack([out_real, out_imag], axis=1)
    returned = lax.all_to_all(
        jnp.einsum("mcqk,ckdx->mdxq", coupled, inverse, precision=highest),
        "lat",
        split_axis=2,
        concat_axis=3,
        tiled=True,
    )
    per_depth = jnp.einsum("js,sdxq->jdxq", onehot, returned, precision=highest)
    cos_back, sin_back = phases(offsets, padded, 1.0)
    turned = rotate(per_depth, cos_back, sin_back)
    result = jnp.einsum("jcxk,ckdy->jdxy", turned, inverse, precision=highest)
    return result * (1.0 / (padded * padded))


def solution(mesh):
    in_specs = (
        P("group", None, "lat", None),
        P("group", None, None, "lat", None),
        P("group"),
        P("group"),
    )
    out_specs = P("group", None, "lat", None)
    n = mesh.shape["lat"]

    def either(currents, green, section_map, offsets):
        fits = 2 * green.shape[3] == LANES and currents.shape[2] % 16 == 0
        if fits and currents.shape[3] % (2 * LANES) == 0:
            return per_device_kernels(n, currents, green, section_map, offsets)
        return per_device(currents, green, section_map, offsets)

    return jax.shard_map(
        either, mesh=mesh, in_specs=in_specs, out_specs=out_specs, check_vma=False
    )
```

profile of v0, /device:TPU:31, one launch (start us, length us, event | category | flops | bytes accessed | tf_op | source)
XLA Modules:
  0.0 127.5 jit_solution(13886471904194796302)
XLA Ops:
  0.0 1.0 sine_multiply_fusion
  1.0 0.0 copy-start
  1.0 2.2 %copy-done = bf16[2,512,2048]{2,1,0:T(8,128)(2,1)S(1)} copy-done((bf16[2,512,2048]{2,1,0:T(8,128)(2,1)S(1)}, bf16[2,512,2048]{2,1,0:T(8,128)(2,1)}, u32[]{:S(2)}) %copy-start) | copy-done | bytes 4194328
  3.2 0.0 copy-start.4
  3.2 1.2 copy-done.4
  4.4 0.0 copy-start.5
  4.4 0.7 copy-done.5
  5.1 7.4 %shard_map.82.src_ref = f32[8,32,2048]{2,1,0:T(8,128)S(1)} custom-call(s32[8]{0:T(128)S(1)} %copy-done.5, f32[8,2,32,512]{3,2,1,0:T(8,128)S(1)} %copy-done.4, bf16[2,512,2048]{2,1,0:T(8,128)(2,1)S(1)} %copy-done, bf16[2,512,2048]{2,1,0:T(8,128)(2,1)S(1)} %copy-done, f32[8,2048]{1,0:T(8,128)S(1)} %get-tuple-element.6.cos_ref, ...), custom_call_target="tpu_custom_call" | custom-call | tf_op jit(solution)/shard_map/pallas_call | solution.py:336
  12.5 0.0 copy-start.3
  12.5 1.3 %copy-done.3 = f32[8,32,2048]{2,1,0:T(8,128)} copy-done((f32[8,32,2048]{2,1,0:T(8,128)}, f32[8,32,2048]{2,1,0:T(8,128)S(1)}, u32[]{:S(2)}) %copy-start.3) | copy-done | bytes 2097176
  13.9 0.0 copy-start.6
  13.9 103.5 %shard_map.83.ret_ref = f32[8,32,2048]{2,1,0:T(8,128)} custom-call(s32[8]{0:T(128)} %map_ref.5, f32[8,32,2048]{2,1,0:T(8,128)} %copy-done.3, f32[8,8,2,64,1024]{4,3,2,1,0:T(8,128)} %green_hbm.1, bf16[2,2,512,1024]{3,2,1,0:T(8,128)(2,1)} %constant.74.clone.table_hbm, bf16[2,2,1024,512]{3,2,1,0:T(8,128)(2,1)} %constant.75.clone.back_hbm), custom_call_target="tpu_custom_call" | custom-call | tf_op jit(solution)/shard_map/pallas_call | solution.py:379
  117.4 0.0 copy-done.6
  117.4 0.0 copy-start.1
  117.4 2.2 %copy-done.1 = bf16[2,2048,512]{2,1,0:T(8,128)(2,1)S(1)} copy-done((bf16[2,2048,512]{2,1,0:T(8,128)(2,1)S(1)}, bf16[2,2048,512]{2,1,0:T(8,128)(2,1)}, u32[]{:S(2)}) %copy-start.1) | copy-done | bytes 4194328
  119.6 0.0 copy-start.2
  119.6 1.6 %copy-done.2 = f32[8,32,2048]{2,1,0:T(8,128)S(1)} copy-done((f32[8,32,2048]{2,1,0:T(8,128)S(1)}, f32[8,32,2048]{2,1,0:T(8,128)}, u32[]{:S(2)}) %copy-start.2) | copy-done | bytes 2097176
  121.2 6.3 %shard_map.84 = f32[8,2,32,512]{3,2,1,0:T(8,128)} custom-call(s32[8]{0:T(128)S(1)} %copy-done.6, f32[8,32,2048]{2,1,0:T(8,128)S(1)} %copy-done.2, bf16[2,2048,512]{2,1,0:T(8,128)(2,1)S(1)} %copy-done.1, bf16[2,2048,512]{2,1,0:T(8,128)(2,1)S(1)} %copy-done.1, f32[8,2048]{1,0:T(8,128)S(1)} %get-tuple-element.6.cos_ref, f32[8,2048]{1,0:T(8,128)S(1)} %get-tuple-element.5.sin_ref), custom_call_target="tpu_custom_call" | custom-call | tf_op jit(solution)/shard_map/pallas_call | solution.py:380
  (2 shorter events, 0.0 us)
Async XLA Ops:
  1.0 2.2 %copy-start = (bf16[2,512,2048]{2,1,0:T(8,128)(2,1)S(1)}, bf16[2,512,2048]{2,1,0:T(8,128)(2,1)}, u32[]{:S(2)}) copy-start(bf16[2,512,2048]{2,1,0:T(8,128)(2,1)} %constant.72.clone.high_ref.low_ref) | copy-start | bytes 12582916
  3.2 1.2 copy-start.4
  4.4 0.7 copy-start.5
  12.5 1.3 %copy-start.3 = (f32[8,32,2048]{2,1,0:T(8,128)}, f32[8,32,2048]{2,1,0:T(8,128)S(1)}, u32[]{:S(2)}) copy-start(f32[8,32,2048]{2,1,0:T(8,128)S(1)} %shard_map.82.src_ref) | copy-start | bytes 6291460
  13.9 103.5 %copy-start.6 = (s32[8]{0:T(128)S(1)}, s32[8]{0:T(128)}, u32[]{:S(2)}) copy-start(s32[8]{0:T(128)} %map_ref.5) | copy-start | bytes 100
  117.4 2.2 %copy-start.1 = (bf16[2,2048,512]{2,1,0:T(8,128)(2,1)S(1)}, bf16[2,2048,512]{2,1,0:T(8,128)(2,1)}, u32[]{:S(2)}) copy-start(bf16[2,2048,512]{2,1,0:T(8,128)(2,1)} %constant.73.clone.high_ref.low_ref) | copy-start | bytes 12582916
  119.6 1.6 %copy-start.2 = (f32[8,32,2048]{2,1,0:T(8,128)S(1)}, f32[8,32,2048]{2,1,0:T(8,128)}, u32[]{:S(2)}) copy-start(f32[8,32,2048]{2,1,0:T(8,128)} %shard_map.83.ret_ref) | copy-start | bytes 6291460
where the time goes:
time: 128 us; the launch traced here: 127 us
  Pallas kernels  117 us (91%)
  local copies, waits for them, and re-layouts  9.18 us (7%)
    pallas_call x1, Pallas kernels, per_device_kernels(): returned = exchange(sections)(section_map, sources, green, table, back)  103 us
    unnamed x14, local copies, waits for them, and re-layouts  9.18 us
    pallas_call x1, Pallas kernels, per_device_kernels(): pl.pallas_call(forward_kernel, grid=(lanes // column,), out_shape=jax.Sha...  7.44 us
    pallas_call x1, Pallas kernels, per_device_kernels(): pl.pallas_call(inverse_kernel, grid=(width // column,), out_shape=jax.Sha...  6.33 us

commit v1 on v0

--- a/solution.py
+++ b/solution.py
@@ -312,10 +312,23 @@
     pltpu.make_async_copy(gone, gone, send_back).wait()
 
 
-def per_device_kernels(n, currents, green, section_map, offsets):
+def most_sections(section_map, groups):
+    bits = lax.reduce(
+        jnp.left_shift(jnp.int32(1), section_map), np.int32(0), lax.bitwise_or, (0,)
+    )
+    count = lax.population_count(bits)
+    most = count
+    for shift in range(1, groups):
+        ring = [(group, (group + shift) % groups) for group in range(groups)]
+        most = jnp.maximum(most, lax.ppermute(count, "group", ring))
+    return most
+
+
+def per_device_kernels(n, groups, currents, green, section_map, offsets):
     depths, _, rows, width = currents.shape
     sections, _, _, block, period = green.shape
     lanes = 2 * period
+    most = most_sections(section_map, groups)
     f32, bf16 = jnp.float32, jnp.bfloat16
     cosine, sine = waves(width, period)
     blocked = blocked_table(width, period, block)
@@ -347,7 +360,10 @@
         ],
         out_specs=pl.BlockSpec((sections, rows, column), lambda i: (0, 0, i)),
         scratch_shapes=[pltpu.VMEM((4 * depths * rows, width), bf16)],
-        compiler_params=pltpu.CompilerParams(vmem_limit_bytes=32 * 2**20),
+        cost_estimate=pl.CostEstimate(
+            flops=12 * depths * rows * width * lanes, bytes_accessed=7 * 2**20, transcendentals=0
+        ),
+        compiler_params=pltpu.CompilerParams(vmem_limit_bytes=limit),
     )(section_map, currents, spread, spread, turn_cos, turn_sin)
 
     def exchange(slots):
@@ -376,7 +392,10 @@
             ),
         )
 
-    returned = exchange(sections)(section_map, sources, green, table, back)
+    fewest = sections // 2 + 1
+    branches = [exchange(slots) for slots in range(fewest, sections + 1)]
+    branch = jnp.clip(most - fewest, 0, sections - fewest)
+    returned = lax.switch(branch, branches, section_map, sources, green, table, back)
     return pl.pallas_call(
         inverse_kernel,
         grid=(width // column,),
@@ -391,7 +410,7 @@
         ],
         out_specs=pl.BlockSpec((depths, 2, rows, column), lambda i: (0, 0, 0, i)),
         scratch_shapes=[pltpu.VMEM((4 * depths * rows, lanes), bf16)],
-        compiler_params=pltpu.CompilerParams(vmem_limit_bytes=40 * 2**20),
+        compiler_params=pltpu.CompilerParams(vmem_limit_bytes=limit),
     )(section_map, returned, gather, gather, turn_cos, turn_sin)
 
 
@@ -471,12 +490,12 @@
         P("group"),
     )
     out_specs = P("group", None, "lat", None)
-    n = mesh.shape["lat"]
+    n, groups = mesh.shape["lat"], mesh.shape["group"]
 
     def either(currents, green, section_map, offsets):
-        fits = 2 * green.shape[3] == LANES and currents.shape[2] % 16 == 0
+        fits = 2 * green.shape[3] == LANES and green.shape[0] < 32 and currents.shape[2] % 16 == 0
         if fits and currents.shape[3] % (2 * LANES) == 0:
-            return per_device_kernels(n, currents, green, section_map, offsets)
+            return per_device_kernels(n, groups, currents, green, section_map, offsets)
         return per_device(currents, green, section_map, offsets)
 
     return jax.shard_map(

time: 128 us -> 93.6 us (0.73)
  the two profiles are of different devices: /device:TPU:31 before, /device:TPU:0 now
where the time goes in v1:
time: 93.6 us; the launch traced here: 93.3 us
  Pallas kernels  84.6 us (90%)
  starting transfers between devices  4.3 us (5%)
  other arithmetic  2.95 us (3%)
  between operations  1.26 us (1%)
    pallas_call x1, Pallas kernels, per_device_kernels(): lax.switch(branch, branches, section_map, sources, green, table, back)  67.9 us
    pallas_call x1, Pallas kernels, per_device_kernels(): pl.pallas_call(forward_kernel, grid=(lanes // column,), out_shape=jax.Sha...  8.81 us
    pallas_call x1, Pallas kernels, per_device_kernels(): pl.pallas_call(inverse_kernel, grid=(width // column,), out_shape=jax.Sha...  7.94 us
    ppermute x1, starting transfers between devices, most_sections(): most = jnp.maximum(most, lax.ppermute(count, 'group', ring))  4.3 us
  transfers between devices with their start and end apart: 1, of which 0 were waited for; matrix products, arithmetic and copies ran while one was open for 2% of the time, Pallas kernels for 9%

profile of v1, /device:TPU:0, one launch (start us, length us, event | category | flops | bytes accessed | tf_op | source)
XLA Modules:
  0.0 93.3 jit_solution(5233075951736566876)
XLA Ops:
  0.0 1.3 %shift-left_reduce_fusion = s32[]{:T(128)} fusion(s32[8]{0:T(128)} %map_ref.3), kind=kLoop, calls=%fused_computation.31 | loop fusion | flops 15 | bytes 36 | tf_op jit(solution)/shard_map/reduce_or | solution.py:316
  2.0 4.3 %collective-permute-start = (s32[]{:T(128)}, s32[]{:T(128)}, u32[]{:S(2)}, u32[]{:S(2)}) collective-permute-start(s32[]{:T(128)} %population_count.3), channel_id=1, source_target_pairs={{0,16},{16,0},{1,17},{17,1},{2,18},{18,2},{3,19},{19,3},{4,20},{20... | collective-permute-start | bytes 20 | tf_op jit(solution)/shard_map/ppermute | solution.py:323
  6.3 1.7 %sine_multiply_fusion = (f32[8,2048]{1,0:T(8,128)}, f32[8,2048]{1,0:T(8,128)}) fusion(f32[2048]{0:T(1024)S(1)} %fusion.18, s32[2048]{0:T(1024)S(1)} %fusion.15, s32[8]{0:T(128)} %param.15), kind=kLoop, calls=%fused_computation.8 | loop fusion | flops 245760 | bytes 147488 | tf_op jit(solution)/shard_map/mul | solution.py:344
  7.9 0.0 copy-start
  7.9 8.8 %shard_map.82 = f32[8,32,2048]{2,1,0:T(8,128)S(1)} custom-call(s32[8]{0:T(128)} %map_ref.3, f32[8,2,32,512]{3,2,1,0:T(8,128)} %cur_ref.1, bf16[2,512,2048]{2,1,0:T(8,128)(2,1)} %constant.79.clone.high_ref.low_ref, bf16[2,512,2048]{2,1,0:T(8,128)(2,1)} %constant.79.clone.high_ref.low_ref, f32[8,2048]{1,0:T(8,128)} %get-tuple-element.71.cos_ref, ...), custom_call_target="tpu_custom_call" | custom-call | flops 3221225472 | bytes 7340032 | tf_op jit(solution)/shard_map/pallas_call | solution.py:349
  16.7 0.0 collective-permute-done
  17.3 0.0 copy-done
  17.3 68.1 %conditional.1 = (f32[8,32,2048]{2,1,0:T(8,128)}) conditional(s32[]{:T(128)} %clamp.3, (s32[8]{0:T(128)S(1)}, f32[8,32,2048]{2,1,0:T(8,128)S(1)}, f32[8,8,2,64,1024]{4,3,2,1,0:T(8,128)}, bf16[2,2,512,1024]{3,2,1,0:T(8,128)(2,1)}, bf16[2,2,1024,512]{3,2,1,0:T(8,128)(2,1)}) %tuple.23, (s32[8]{0:T(128)S(1)}, ...), branch_computations={%region_1.2_spmd, %region_2.3_spmd, %region_3.4_spmd, %region_4.5_... | conditional | bytes 8 | solution.py:398
  17.3 67.9 %branch_0_fun.1 = f32[8,32,2048]{2,1,0:T(8,128)} custom-call(s32[8]{0:T(128)S(1)} %get-tuple-element.48.map_ref, f32[8,32,2048]{2,1,0:T(8,128)S(1)} %get-tuple-element.50.src_ref, f32[8,8,2,64,1024]{4,3,2,1,0:T(8,128)} %get-tuple-element.52.green_hbm, bf16[2,2,512,1024]{3,2,1,0:T(8,128)(2,1)} %get-tuple-element.53.table_hbm, ...), custom_call_target="tpu_custom_call" | custom-call | tf_op jit(solution)/shard_map/cond/branch_0_fun/pallas_call | solution.py:398
  85.4 7.9 %shard_map.83 = f32[8,2,32,512]{3,2,1,0:T(8,128)} custom-call(s32[8]{0:T(128)S(1)} %copy-done, f32[8,32,2048]{2,1,0:T(8,128)} %get-tuple-element.72.ret_ref, bf16[2,2048,512]{2,1,0:T(8,128)(2,1)} %constant.80.clone.high_ref.low_ref, bf16[2,2048,512]{2,1,0:T(8,128)(2,1)} %constant.80.clone.high_ref.low_ref, f32[8,2048]{1,0:T(8,128)} %get-tuple-element.71.cos_ref, ...), custom_call_target="tpu_custom_call" | custom-call | tf_op jit(solution)/shard_map/pallas_call | solution.py:399
  (2 shorter events, 0.0 us)
Async XLA Ops:
  2.0 14.8 %collective-permute-start = (s32[]{:T(128)}, s32[]{:T(128)}, u32[]{:S(2)}, u32[]{:S(2)}) collective-permute-start(s32[]{:T(128)} %population_count.3), channel_id=1, source_target_pairs={{0,16},{16,0},{1,17},{17,1},{2,18},{18,2},{3,19},{19,3},{4,20},{20... | collective-permute-start | bytes 20 | tf_op jit(solution)/shard_map/ppermute | solution.py:323
  7.9 9.4 %copy-start = (s32[8]{0:T(128)S(1)}, s32[8]{0:T(128)}, u32[]{:S(2)}) copy-start(s32[8]{0:T(128)} %map_ref.3) | copy-start | bytes 100

commit v2 on v1

--- a/solution.py
+++ b/solution.py
@@ -74,34 +74,6 @@
     for section, place in enumerate(rank):
         value = jnp.where(map_ref[depth] == section, place, value)
     return value
-
-
-def forward_kernel(map_ref, cur_ref, high_ref, low_ref, cos_ref, sin_ref, out_ref, split_ref):
-    depths, _, rows, width = cur_ref.shape
-    sections = out_ref.shape[0]
-    half = depths * rows
-
-    @pl.when(pl.program_id(0) == 0)
-    def _():
-        for part in range(2):
-            high, low = split_bf16(cur_ref[:, part].reshape(half, width))
-            split_ref[pl.ds(part * half, half), :] = high
-            split_ref[pl.ds((2 + part) * half, half), :] = low
-
-    product = dot_split(split_ref[...], high_ref[...], low_ref[...])
-    lane = lax.broadcasted_iota(jnp.int32, (1, product.shape[1]), 1) % LANES
-    sign = jnp.where(lane < LANES // 2, -1.0, 1.0)
-    spectrum = product[:half] + swap_halves(product[half:]) * sign
-    swapped = swap_halves(spectrum)
-    rank, _ = section_slots(map_ref, depths, sections)
-    out_ref[...] = jnp.zeros_like(out_ref)
-    for depth in range(depths):
-        span = slice(depth * rows, (depth + 1) * rows)
-        turned = (
-            spectrum[span] * cos_ref[pl.ds(depth, 1), :]
-            + swapped[span] * sin_ref[pl.ds(depth, 1), :]
-        )
-        out_ref[slot_of_depth(map_ref, rank, depth)] += turned
 
 
 def inverse_kernel(map_ref, ret_ref, high_ref, low_ref, cos_ref, sin_ref, out_ref, split_ref):
@@ -136,8 +108,8 @@
 
 
 def exchange_kernel(
-    n, slots, map_ref, src_ref, green_hbm, table_hbm, back_hbm, out_ref,
-    recv, green, table, back, spectra, total, result,
+    n, slots, map_ref, cos_ref, sin_ref, cur_hbm, spread_hbm, green_hbm, table_hbm, back_hbm,
+    out_ref, cur, spread, split_ref, src_ref, recv, green, table, back, spectra, total, result,
     send_sem, recv_sem, send_back, recv_back, load_sem, green_sem,
 ):
     group = lax.axis_index("group")
@@ -148,6 +120,10 @@
     tables_in = pltpu.make_async_copy(table_hbm, table, load_sem.at[0])
     back_in = pltpu.make_async_copy(back_hbm, back, load_sem.at[1])
     green_in = pltpu.make_async_copy(green_hbm, green, green_sem)
+    cur_in = pltpu.make_async_copy(cur_hbm, cur, load_sem.at[2])
+    spread_in = pltpu.make_async_copy(spread_hbm, spread, load_sem.at[3])
+    cur_in.start()
+    spread_in.start()
     tables_in.start()
 
     barrier = pltpu.get_barrier_semaphore()
@@ -158,30 +134,46 @@
         return carry
 
     lax.fori_loop(1, n, greet, 0)
+    depths, part_width = cur.shape[0], cur.shape[3]
+    half = depths * rows
+    cur_in.wait()
+    for part in range(2):
+        high, low = split_bf16(cur[:, part].reshape(half, part_width))
+        split_ref[pl.ds(part * half, half), :] = high
+        split_ref[pl.ds((2 + part) * half, half), :] = low
+    spread_in.wait()
     pl.semaphore_wait(barrier, n - 1)
 
     my_rows = pl.ds(pl.multiple_of(me * rows, rows), rows)
     my_lanes = pl.ds(pl.multiple_of(me * LANES, LANES), LANES)
 
-    def send_sources(base, count):
+    def send_source(base, count, other):
         batch = pl.ds(base, count)
-        pltpu.make_async_copy(
-            src_ref.at[batch, :, my_lanes], recv.at[batch, my_rows], recv_sem.at[base // 2]
-        ).start()
-
-        def send(step, carry):
-            other = lax.rem(me + step, n)
+        lanes_there = pl.ds(pl.multiple_of(other * LANES, LANES), LANES)
+
+        @pl.when(other != me)
+        def _():
             pltpu.make_async_remote_copy(
-                src_ref=src_ref.at[batch, :, pl.ds(pl.multiple_of(other * LANES, LANES), LANES)],
+                src_ref=src_ref.at[batch, :, lanes_there],
                 dst_ref=recv.at[batch, my_rows],
                 send_sem=send_sem,
                 recv_sem=recv_sem.at[base // 2],
                 device_id=(group, other),
                 device_id_type=MESH,
             ).start()
+
+        @pl.when(other == me)
+        def _():
+            pltpu.make_async_copy(
+                src_ref.at[batch, :, my_lanes], recv.at[batch, my_rows], recv_sem.at[base // 2]
+            ).start()
+
+    def send_sources(base, count):
+        def send(step, carry):
+            send_source(base, count, lax.rem(me + n // 2 + step, n))
             return carry
 
-        lax.fori_loop(1, n, send, 0)
+        lax.fori_loop(0, n, send, 0)
 
     def send_results(base, count):
         batch = pl.ds(base, count)
@@ -190,7 +182,7 @@
         ).start()
 
         def send(step, carry):
-            other = lax.rem(me + step, n)
+            other = lax.rem(me + 1 + lax.rem(n // 2 + step, n - 1), n)
             pltpu.make_async_remote_copy(
                 src_ref=result.at[batch, pl.ds(pl.multiple_of(other * rows, rows), rows)],
                 dst_ref=out_ref.at[batch, :, my_lanes],
@@ -201,29 +193,61 @@
             ).start()
             return carry
 
-        lax.fori_loop(1, n, send, 0)
-
-    def batches(body):
+        lax.fori_loop(0, n - 1, send, 0)
+
+    def batches(body, first=0):
         def pair(index, carry):
             body(index * 2, 2)
             return carry
 
-        lax.fori_loop(0, slots // 2, pair, 0)
+        lax.fori_loop(first, slots // 2, pair, 0)
         if slots % 2:
             body(slots - 1, 1)
 
-    batches(send_sources)
     green_in.start()
     back_in.start()
-
     rank, used = section_slots(map_ref, map_ref.shape[0], sections)
     place = []
     for slot in range(slots):
-        found = jnp.int32(0)
+        found = jnp.int32(-1)
         for section in range(sections):
             here = jnp.logical_and(rank[section] == slot, used[section] == 1)
             found = jnp.where(here, section, found)
         place.append(found)
+
+    chunk = 2 * LANES
+    weights = [
+        [jnp.where(map_ref[depth] == place[slot], 1.0, 0.0) for depth in range(depths)]
+        for slot in range(slots)
+    ]
+    place = [jnp.maximum(found, 0) for found in place]
+
+    def transform(index, carry):
+        column = lax.rem(me // 2 + n // 4 + index, n // 2)
+        span = pl.ds(pl.multiple_of(column * chunk, chunk), chunk)
+        product = dot_split(split_ref[...], spread[0, :, span], spread[1, :, span])
+        lane = lax.broadcasted_iota(jnp.int32, (1, chunk), 1) % LANES
+        sign = jnp.where(lane < LANES // 2, -1.0, 1.0)
+        spectrum = product[:half] + swap_halves(product[half:]) * sign
+        swapped = swap_halves(spectrum)
+        turned = []
+        for depth in range(depths):
+            at = slice(depth * rows, (depth + 1) * rows)
+            turned.append(
+                spectrum[at] * cos_ref[pl.ds(depth, 1), span]
+                + swapped[at] * sin_ref[pl.ds(depth, 1), span]
+            )
+        for slot in range(slots):
+            summed = turned[0] * weights[slot][0]
+            for depth in range(1, depths):
+                summed = summed + turned[depth] * weights[slot][depth]
+            src_ref[slot, :, span] = summed
+        send_source(0, 2, column * 2)
+        send_source(0, 2, column * 2 + 1)
+        return carry
+
+    lax.fori_loop(0, n // 2, transform, 0)
+    batches(send_sources, 1)
 
     def place_of(slot):
         found = place[0]
@@ -233,7 +257,6 @@
 
     total[...] = jnp.zeros_like(total)
     tables_in.wait()
-    chunk = 2 * LANES
 
     def take(base, count):
         arrived = recv.at[pl.ds(base, count)]
@@ -345,34 +368,19 @@
     limit = 60 * 2**20
     smem = pl.BlockSpec(memory_space=pltpu.SMEM)
     anywhere = pl.BlockSpec(memory_space=pl.ANY)
+    whole = pl.BlockSpec(memory_space=pltpu.VMEM)
     column = 2 * LANES
-    sources = pl.pallas_call(
-        forward_kernel,
-        grid=(lanes // column,),
-        out_shape=jax.ShapeDtypeStruct((sections, rows, lanes), f32),
-        in_specs=[
-            smem,
-            pl.BlockSpec((depths, 2, rows, width), lambda i: (0, 0, 0, 0)),
-            pl.BlockSpec((None, width, column), lambda i: (0, 0, i)),
-            pl.BlockSpec((None, width, column), lambda i: (1, 0, i)),
-            pl.BlockSpec((depths, column), lambda i: (0, i)),
-            pl.BlockSpec((depths, column), lambda i: (0, i)),
-        ],
-        out_specs=pl.BlockSpec((sections, rows, column), lambda i: (0, 0, i)),
-        scratch_shapes=[pltpu.VMEM((4 * depths * rows, width), bf16)],
-        cost_estimate=pl.CostEstimate(
-            flops=12 * depths * rows * width * lanes, bytes_accessed=7 * 2**20, transcendentals=0
-        ),
-        compiler_params=pltpu.CompilerParams(vmem_limit_bytes=limit),
-    )(section_map, currents, spread, spread, turn_cos, turn_sin)
-
     def exchange(slots):
         return pl.pallas_call(
             functools.partial(exchange_kernel, n, slots),
             out_shape=jax.ShapeDtypeStruct((sections, rows, lanes), f32),
-            in_specs=[smem] + [anywhere] * 4,
+            in_specs=[smem, whole, whole] + [anywhere] * 5,
             out_specs=anywhere,
             scratch_shapes=[
+                pltpu.VMEM(currents.shape, f32),
+                pltpu.VMEM(spread.shape, bf16),
+                pltpu.VMEM((4 * depths * rows, width), bf16),
+                pltpu.VMEM((slots, rows, lanes), f32),
                 pltpu.VMEM((slots, width, LANES), f32),
                 pltpu.VMEM(green.shape, f32),
                 pltpu.VMEM(table.shape, bf16),
@@ -384,7 +392,7 @@
                 pltpu.SemaphoreType.DMA(((slots + 1) // 2,)),
                 pltpu.SemaphoreType.DMA,
                 pltpu.SemaphoreType.DMA,
-                pltpu.SemaphoreType.DMA((2,)),
+                pltpu.SemaphoreType.DMA((4,)),
                 pltpu.SemaphoreType.DMA,
             ],
             compiler_params=pltpu.CompilerParams(
@@ -395,7 +403,9 @@
     fewest = sections // 2 + 1
     branches = [exchange(slots) for slots in range(fewest, sections + 1)]
     branch = jnp.clip(most - fewest, 0, sections - fewest)
-    returned = lax.switch(branch, branches, section_map, sources, green, table, back)
+    returned = lax.switch(
+        branch, branches, section_map, turn_cos, turn_sin, currents, spread, green, table, back
+    )
     return pl.pallas_call(
         inverse_kernel,
         grid=(width // column,),
@@ -493,7 +503,7 @@
     n, groups = mesh.shape["lat"], mesh.shape["group"]
 
     def either(currents, green, section_map, offsets):
-        fits = 2 * green.shape[3] == LANES and green.shape[0] < 32 and currents.shape[2] % 16 == 0
+        fits = 2 * green.shape[3] == LANES and green.shape[0] < 32 and currents.shape[2] % 16 == 0 and n % 4 == 0
         if fits and currents.shape[3] % (2 * LANES) == 0:
             return per_device_kernels(n, groups, currents, green, section_map, offsets)
         return per_device(currents, green, section_map, offsets)

time: 93.6 us -> 87.4 us (0.934)
  Pallas kernels: 84.6 us -> 79.1 us
    pallas_call x2 -> x1, Pallas kernels: 76.7 us -> 71.9 us  [per_device_kernels(): lax.switch(branch, branches, section_map, turn_cos, turn_sin, currents, s...]
  transfers between devices with their start and end apart: 1 -> 1, of which waited for: 0 -> 0; matrix products, arithmetic and copies ran while one was open for 2% -> 1% of each run, Pallas kernels for 9% -> 0%
where the time goes in v2:
time: 87.4 us; the launch traced here: 87.2 us
  Pallas kernels  79.1 us (91%)
  starting transfers between devices  4.3 us (5%)
  other arithmetic  2.3 us (3%)
  between operations  1.32 us (2%)
    pallas_call x1, Pallas kernels, per_device_kernels(): lax.switch(branch, branches, section_map, turn_cos, turn_sin, currents, s...  71.9 us
    pallas_call x1, Pallas kernels, per_device_kernels(): pl.pallas_call(inverse_kernel, grid=(width // column,), out_shape=jax.Sha...  7.2 us
    ppermute x1, starting transfers between devices, most_sections(): most = jnp.maximum(most, lax.ppermute(count, 'group', ring))  4.3 us
  transfers between devices with their start and end apart: 1, of which 0 were waited for; matrix products, arithmetic and copies ran while one was open for 1% of the time, Pallas kernels for 0%

profile of v2, /device:TPU:0, one launch (start us, length us, event | category | flops | bytes accessed | tf_op | source)
XLA Modules:
  0.0 87.2 jit_solution(7106694264156632041)
XLA Ops:
  0.0 1.3 %shift-left_reduce_fusion = s32[]{:T(128)} fusion(s32[8]{0:T(128)} %map_ref.1), kind=kLoop, calls=%fused_computation.31 | loop fusion | flops 15 | bytes 36 | tf_op jit(solution)/shard_map/reduce_or | solution.py:339
  2.0 4.3 %collective-permute-start = (s32[]{:T(128)}, s32[]{:T(128)}, u32[]{:S(2)}, u32[]{:S(2)}) collective-permute-start(s32[]{:T(128)} %population_count.3), channel_id=1, source_target_pairs={{0,16},{16,0},{1,17},{17,1},{2,18},{18,2},{3,19},{19,3},{4,20},{20... | collective-permute-start | bytes 20 | tf_op jit(solution)/shard_map/ppermute | solution.py:346
  6.3 1.0 %sine_multiply_fusion = (f32[8,2048]{1,0:T(8,128)S(1)}, f32[8,2048]{1,0:T(8,128)S(1)}) fusion(f32[2048]{0:T(1024)S(1)} %fusion.18, s32[2048]{0:T(1024)S(1)} %fusion.15, s32[8]{0:T(128)} %param.15), kind=kLoop, calls=%fused_computation.8 | loop fusion | flops 245760 | bytes 147488 | tf_op jit(solution)/shard_map/mul | solution.py:367
  7.3 0.0 collective-permute-done
  7.9 72.1 %conditional.1 = (f32[8,32,2048]{2,1,0:T(8,128)S(1)}) conditional(s32[]{:T(128)} %clamp.3, (s32[8]{0:T(128)}, f32[8,2048]{1,0:T(8,128)S(1)}, f32[8,2048]{1,0:T(8,128)S(1)}, f32[8,2,32,512]{3,2,1,0:T(8,128)}, bf16[2,512,2048]{2,1,0:T(8,128)(2,1)}, /*index=5*/f32[8,8,2,64,1024]{4,3,2,1,0:T(8,128)}, ...), branch_computations={%region_1.2_spmd, %region_2.3_spmd, %region_3.4_spmd, %region_4.5_... | conditional | bytes 8 | solution.py:406
  7.9 71.9 %branch_0_fun.1 = f32[8,32,2048]{2,1,0:T(8,128)S(1)} custom-call(s32[8]{0:T(128)} %get-tuple-element.72.map_ref, f32[8,2048]{1,0:T(8,128)S(1)} %get-tuple-element.74.cos_ref, f32[8,2048]{1,0:T(8,128)S(1)} %get-tuple-element.76.sin_ref, f32[8,2,32,512]{3,2,1,0:T(8,128)} %get-tuple-element.77.cur_hbm, bf16[2,512,2048]{2,1,0:T(8,128)(2,1)} %get-tuple-element.78.spread_hbm, ...), custom_call_target="tpu_custom_call" | custom-call | tf_op jit(solution)/shard_map/cond/branch_0_fun/pallas_call | solution.py:406
  80.0 7.2 %shard_map.82 = f32[8,2,32,512]{3,2,1,0:T(8,128)} custom-call(s32[8]{0:T(128)} %map_ref.1, f32[8,32,2048]{2,1,0:T(8,128)S(1)} %get-tuple-element.108.ret_ref, bf16[2,2048,512]{2,1,0:T(8,128)(2,1)} %constant.80.clone.high_ref.low_ref, bf16[2,2048,512]{2,1,0:T(8,128)(2,1)} %constant.80.clone.high_ref.low_ref, f32[8,2048]{1,0:T(8,128)S(1)} %get-tuple-element.107.cos_ref, ...), custom_call_target="tpu_custom_call" | custom-call | tf_op jit(solution)/shard_map/pallas_call | solution.py:409
  (2 shorter events, 0.0 us)
Async XLA Ops:
  2.0 5.3 %collective-permute-start = (s32[]{:T(128)}, s32[]{:T(128)}, u32[]{:S(2)}, u32[]{:S(2)}) collective-permute-start(s32[]{:T(128)} %population_count.3), channel_id=1, source_target_pairs={{0,16},{16,0},{1,17},{17,1},{2,18},{18,2},{3,19},{19,3},{4,20},{20... | collective-permute-start | bytes 20 | tf_op jit(solution)/shard_map/ppermute | solution.py:346
